TPU v7x, 32 devices: a whole 2x2x4 slice. The times are simulated.
32 devices in a mesh: ctx: 16 (over z, x, core), tp: 2 (over y).
Axes of the slice: x: 2, y: 2, z: 4, core: 2. Of those that a mesh axis runs over, the one named last changes fastest.
Arguments:
- queries: bfloat16 [4096, 8192], P('ctx', 'tp'), may hold values from -6 to 6
- key_vectors: bfloat16 [4096, 1024], P(('ctx', 'tp')), may hold values from -6 to 6
- value_vectors: bfloat16 [4096, 1024], P(('ctx', 'tp')), may hold values from -6 to 6
- output_gradient: bfloat16 [4096, 8192], P('ctx', 'tp'), may hold values from -6 to 6
- doc_lengths: int32 [8], replicated, may hold values from 1 to 1793, 4096 in all
Outputs:
- attn_output: bfloat16 [4096, 8192], P('ctx', 'tp')
- grad_queries: bfloat16 [4096, 8192], P('ctx', 'tp')
- key_gradient: bfloat16 [4096, 1024], P(('ctx', 'tp'))
- value_gradient: bfloat16 [4096, 1024], P(('ctx', 'tp'))
All inputs are finite; a program needn't handle non-finite values.
Results may differ from a plain program's by a relative error of at most 0.02.
Values may be sent and summed in bfloat16 or wider, within the bound.
No kernel may reach another device: no remote copies, remote signals or barrier semaphores. Data moves between devices by JAX's collectives and lax.ppermute only.
A program may use at most 128 MiB of HBM per device.

v0:
```python
from functools import partial
import math

import jax
import jax.numpy as jnp
from jax import lax
from jax.sharding import PartitionSpec as P

HEAD_SIZE = 128
WINDOW = 8


def shifted(value, axis, steps):
    count = lax.axis_size(axis)
    leading, last = (max(0, -steps), min(count, count - steps))
    return lax.ppermute(value, axis, [(source, source + steps) for source in range(leading, last)])


def for_sending(array):

    def short(part):
        return part.astype(jnp.bfloat16) if part.dtype == jnp.float32 else part

    return jax.tree.map(short, array)


def doc_index_of(positions, doc_starts):
    above = (positions[:, None] >= doc_starts[None, :]).astype(jnp.int32)
    return jnp.sum(above, axis=1) - 1


def attend_block(block_q, block_g, key_block, value_block, allowed, score_scale):
    scores = (
        jnp.einsum("thd,kd->htk", block_q, key_block, preferred_element_type=jnp.float32)
        * score_scale
    )
    scores = jnp.where(allowed[None], scores, -1e30)
    row_top = jnp.max(scores, axis=2, keepdims=True)
    row_total = jnp.sum(jnp.exp(scores - row_top), axis=2, keepdims=True)
    log_total = row_top + jnp.log(row_total)
    weights = jnp.exp(scores - log_total)
    weights_low = weights.astype(jnp.bfloat16)
    output = jnp.einsum(
        "htk,kd->thd", weights_low, value_block, preferred_element_type=jnp.float32
    ).astype(jnp.bfloat16)
    row_delta = jnp.sum(output.astype(jnp.float32) * block_g.astype(jnp.float32), axis=2)
    row_delta = jnp.transpose(row_delta)[:, :, None]
    grad_weights = jnp.einsum(
        "thd,kd->htk", block_g, value_block, preferred_element_type=jnp.float32
    )
    grad_scores = (weights * (grad_weights - row_delta) * score_scale).astype(jnp.bfloat16)
    grad_query = jnp.einsum(
        "htk,kd->thd", grad_scores, key_block, preferred_element_type=jnp.float32
    ).astype(jnp.bfloat16)
    grad_key = jnp.einsum("htk,thd->kd", grad_scores, block_q, preferred_element_type=jnp.float32)
    grad_value = jnp.einsum("htk,thd->kd", weights_low, block_g, preferred_element_type=jnp.float32)
    return (output, grad_query, grad_key, grad_value)


def body(queries, key_vectors, value_vectors, output_gradient, doc_lengths):
    ctx_index = lax.axis_index("ctx")
    k_heads, v_heads = (
        lax.all_to_all(key_vectors, "tp", split_axis=1, concat_axis=0, tiled=True),
        lax.all_to_all(value_vectors, "tp", split_axis=1, concat_axis=0, tiled=True),
    )
    shard_len = queries.shape[0]
    kv_groups = k_heads.shape[1] // HEAD_SIZE
    row_goal = max(1, 512 // shard_len)
    score_scale = 1.0 / math.sqrt(HEAD_SIZE)
    kv_local = jnp.concatenate([k_heads, v_heads], axis=1)
    feature_count = kv_local.shape[1]
    slot_list = [kv_local]
    for offset in range(1, WINDOW):
        slot_list.append(shifted(kv_local, "ctx", offset))
    window = jnp.stack(slot_list, axis=0)
    doc_starts = jnp.cumsum(doc_lengths, dtype=jnp.int32) - doc_lengths
    local_pos = jnp.arange(shard_len, dtype=jnp.int32)
    slot_index = jnp.arange(WINDOW, dtype=jnp.int32)

    def compute_window(slot_count, q_set, g_set, win, layout):
        query_pos, query_doc, key_pos, key_doc, needed = layout
        local_heads = q_set.shape[1] // HEAD_SIZE // kv_groups
        head_block = max(
            [
                candidate
                for candidate in range(1, local_heads + 1)
                if local_heads % candidate == 0 and candidate <= row_goal
            ]
        )
        per_group = local_heads // head_block
        block_total = kv_groups * per_group
        key_total_count = slot_count * shard_len
        allowed = (query_doc[:, None] == key_doc[None, :key_total_count]) & (
            key_pos[None, :key_total_count] <= query_pos[:, None]
        )
        flat_window = win[:slot_count].reshape(key_total_count, feature_count)

        def one_block(number, buffers):
            out_buf, grad_q_buf, grad_window = buffers
            group_index = number // per_group
            column = (group_index * local_heads + number % per_group * head_block) * HEAD_SIZE
            block_q = lax.dynamic_slice_in_dim(q_set, column, head_block * HEAD_SIZE, 1).reshape(
                shard_len, head_block, HEAD_SIZE
            )
            block_g = lax.dynamic_slice_in_dim(g_set, column, head_block * HEAD_SIZE, 1).reshape(
                shard_len, head_block, HEAD_SIZE
            )
            key_col = group_index * HEAD_SIZE
            value_col = (kv_groups + group_index) * HEAD_SIZE
            key_block = lax.dynamic_slice_in_dim(flat_window, key_col, HEAD_SIZE, 1)
            value_block = lax.dynamic_slice_in_dim(flat_window, value_col, HEAD_SIZE, 1)
            output, grad_query, grad_key, grad_value = attend_block(
                block_q, block_g, key_block, value_block, allowed, score_scale
            )
            out_buf = lax.dynamic_update_slice_in_dim(
                out_buf, output.reshape(shard_len, head_block * HEAD_SIZE), column, 1
            )
            grad_q_buf = lax.dynamic_update_slice_in_dim(
                grad_q_buf, grad_query.reshape(shard_len, head_block * HEAD_SIZE), column, 1
            )
            grad_window = lax.dynamic_update_slice_in_dim(
                grad_window,
                lax.dynamic_slice_in_dim(grad_window, key_col, HEAD_SIZE, 1) + grad_key,
                key_col,
                1,
            )
            grad_window = lax.dynamic_update_slice_in_dim(
                grad_window,
                lax.dynamic_slice_in_dim(grad_window, value_col, HEAD_SIZE, 1) + grad_value,
                value_col,
                1,
            )
            return (out_buf, grad_q_buf, grad_window)

        initial_state = (
            jnp.zeros_like(q_set),
            jnp.zeros_like(q_set),
            jnp.zeros((key_total_count, feature_count), jnp.float32),
        )
        out_buf, grad_q_buf, grad_window = lax.fori_loop(0, block_total, one_block, initial_state)
        grad_window = grad_window.reshape(slot_count, shard_len, feature_count)
        if slot_count < WINDOW:
            grad_window = jnp.concatenate(
                [
                    grad_window,
                    jnp.zeros((WINDOW - slot_count, shard_len, feature_count), jnp.float32),
                ],
                axis=0,
            )
        return (out_buf, grad_q_buf, grad_window)

    first_pos = ctx_index * shard_len
    query_pos = first_pos + local_pos
    query_doc = doc_index_of(query_pos, doc_starts)
    key_pos = ((ctx_index - slot_index)[:, None] * shard_len + local_pos[None, :]).reshape(-1)
    key_doc = doc_index_of(key_pos, doc_starts)
    doc_start = jnp.max(jnp.where(doc_starts <= first_pos, doc_starts, 0))
    needed = jnp.clip(ctx_index - doc_start // shard_len + 1, 1, WINDOW)
    layout = (query_pos, query_doc, key_pos, key_doc, needed)
    branches = [partial(compute_window, count_slots) for count_slots in range(1, WINDOW + 1)]
    out_heads, dq_heads, grad_window = lax.switch(
        layout[4] - 1, branches, queries, output_gradient, window, layout
    )
    grad_own = grad_window[0]
    for offset in range(1, WINDOW):
        grad_own = grad_own + shifted(for_sending(grad_window[offset]), "ctx", -offset)
    grad_k_heads = grad_own[:, : kv_groups * HEAD_SIZE].astype(jnp.bfloat16)
    grad_v_heads = grad_own[:, kv_groups * HEAD_SIZE :].astype(jnp.bfloat16)
    key_gradient, value_gradient = (
        lax.all_to_all(grad_k_heads, "tp", split_axis=0, concat_axis=1, tiled=True),
        lax.all_to_all(grad_v_heads, "tp", split_axis=0, concat_axis=1, tiled=True),
    )
    return (out_heads, dq_heads, key_gradient, value_gradient)


def solution(mesh):
    return jax.shard_map(
        body,
        mesh=mesh,
        in_specs=(
            P("ctx", "tp"),
            P(("ctx", "tp"), None),
            P(("ctx", "tp"), None),
            P("ctx", "tp"),
            P(),
        ),
        out_specs=(P("ctx", "tp"), P("ctx", "tp"), P(("ctx", "tp"), None), P(("ctx", "tp"), None)),
        check_vma=False,
    )
```

profile of v0, /device:TPU:18, one launch (start us, length us, event | category | flops | bytes accessed | tf_op | source)
XLA Modules:
  0.0 675.2 jit_solution(4151459243445339606)
XLA Ops:
  2.3 3.4 all-to-all-start
  11.2 3.4 all-to-all-start.1
  17.4 2.3 all-to-all-done.1
  21.8 3.5 collective-permute-start.1
  28.5 2.5 collective-permute-start.2
  31.9 14.1 %collective-permute-done = bf16[256,1024]{1,0:T(8,128)(2,1)S(1)} collective-permute-done((bf16[256,1024]{1,0:T(8,128)(2,1)S(1)}, bf16[256,1024]{1,0:T(8,128)(2,1)S(1)}, u32[]{:S(2)}, u32[]{:S(2)}) %collective-permute-start) | collective-permute-done | bytes 524320 | tf_op jit(solution)/shard_map/ppermute | solution.py:16
  46.0 5.7 collective-permute-start.3
  52.5 2.9 collective-permute-done.1
  57.6 48.8 %collective-permute-done.2 = bf16[256,1024]{1,0:T(8,128)(2,1)S(1)} collective-permute-done((bf16[256,1024]{1,0:T(8,128)(2,1)S(1)}, bf16[256,1024]{1,0:T(8,128)(2,1)S(1)}, u32[]{:S(2)}, u32[]{:S(2)}) %collective-permute-start.2) | collective-permute-done | bytes 524320 | tf_op jit(solution)/shard_map/ppermute | solution.py:16
  107.2 4.3 collective-permute-done.3
  114.9 308.3 %conditional.1 = (bf16[256,4096]{0,1:T(8,128)(2,1)}, bf16[256,4096]{0,1:T(8,128)(2,1)}, f32[8,256,1024]{2,1,0:T(8,128)}) conditional(s32[]{:T(128)} %clamp.3, (s32[256]{0:T(256)S(1)}, s32[2048]{0:T(1024)S(1)}, s32[2048]{0:T(1024)S(1)}, s32[256]{0:T(256)S(1)}, bf16[256,1024]{1,0:T(8,128)(2,1)S(1)}, ...), branch_computations={%region_4.10_spmd, %region_10.16_spmd, %region_16.22_spmd, %region... | conditional | flops 1627784192 | bytes 104110888 | solution.py:161
  115.1 3.1 slice.77
  121.1 2.5 broadcast.255
  123.6 283.9 %while.155 = (s32[]{:T(128)}, bf16[256,4096]{0,1:T(8,128)(2,1)}, bf16[256,4096]{0,1:T(8,128)(2,1)}, f32[1024,1024]{1,0:T(8,128)}, bf16[1024,1024]{1,0:T(8,128)(2...) while((s32[]{:T(128)}, bf16[256,4096]{0,1:T(8,128)(2,1)}, ...), condition=%wide.region_27.27_spmd.clone, body=%wide.region_23.26_spmd.clone.sunk | while | flops 814087168 | bytes 24019476 | solution.py:140
  127.7 4.0 copy.599
  136.0 2.3 fusion.436
  145.5 4.0 copy.599
  163.2 4.0 copy.599
  171.5 2.3 fusion.436
  180.9 4.0 copy.599
  198.7 4.0 copy.599
  216.4 4.0 copy.599
  234.1 4.0 copy.599
  251.8 4.0 copy.599
  269.6 4.0 copy.599
  277.8 2.3 fusion.436
  287.3 4.0 copy.599
  295.6 2.3 fusion.436
  305.0 4.0 copy.599
  322.8 4.0 copy.599
  340.5 4.0 copy.599
  348.8 2.4 fusion.436
  358.3 4.0 copy.599
  366.6 2.4 fusion.436
  376.1 4.0 copy.599
  384.3 2.4 fusion.436
  393.8 4.0 copy.599
  402.1 2.4 fusion.436
  407.5 6.7 concatenate.19
  423.2 4.0 convert.13
  436.1 34.9 %collective-permute-done.7 = bf16[256,1024]{1,0:T(8,128)(2,1)S(1)} collective-permute-done((bf16[256,1024]{1,0:T(8,128)(2,1)S(1)}, bf16[256,1024]{1,0:T(8,128)(2,1)S(1)}, u32[]{:S(2)}, u32[]{:S(2)}) %collective-permute-start.7) | collective-permute-done | bytes 524320 | tf_op jit(solution)/shard_map/ppermute | solution.py:16
  472.9 147.3 %collective-permute-start.8 = (bf16[256,1024]{1,0:T(8,128)(2,1)S(1)}, bf16[256,1024]{1,0:T(8,128)(2,1)S(1)}, u32[]{:S(2)}, u32[]{:S(2)}) collective-permute-start(bf16[256,1024]{1,0:T(8,128)(2,1)S(1)} %get-tuple-element.2568), channel_id=1, source_target_pairs={{4,0},{6,2},{8,4},{10,6},{12,8},{14,10},{16,12},{18,14},{20,16},{2... | collective-permute-start | bytes 1572872 | tf_op jit(solution)/shard_map/ppermute | solution.py:16
  620.2 19.1 %collective-permute-done.11 = bf16[256,1024]{1,0:T(8,128)(2,1)S(1)} collective-permute-done((bf16[256,1024]{1,0:T(8,128)(2,1)S(1)}, bf16[256,1024]{1,0:T(8,128)(2,1)S(1)}, u32[]{:S(2)}, u32[]{:S(2)}) %collective-permute-start.11) | collective-permute-done | bytes 524320 | tf_op jit(solution)/shard_map/ppermute | solution.py:16
  639.3 11.4 %collective-permute-done.10 = bf16[256,1024]{1,0:T(8,128)(2,1)S(1)} collective-permute-done((bf16[256,1024]{1,0:T(8,128)(2,1)S(1)}, bf16[256,1024]{1,0:T(8,128)(2,1)S(1)}, u32[]{:S(2)}, u32[]{:S(2)}) %collective-permute-start.10) | collective-permute-done | bytes 524320 | tf_op jit(solution)/shard_map/ppermute | solution.py:16
  653.5 7.6 %all_to_all.76 = bf16[2,128,512]{2,1,0:T(8,128)(2,1)S(1)} all-to-all(bf16[2,128,512]{2,1,0:T(8,128)(2,1)S(1)} %bitcast.956), channel_id=1, replica_groups=mesh['ctx'=16,'tp'=2] {'tp'}, dimensions={0} | all-to-all | bytes 524288 | tf_op jit(solution)/shard_map/all_to_all | solution.py:170
  661.1 3.4 all-to-all-start.3
  664.5 4.1 copy.453
  668.6 4.1 copy.454
  (272 shorter events, 239.8 us)
Async XLA Ops:
  2.3 8.9 %all-to-all-start = ((bf16[128,2,512]{2,0,1:T(8,128)(2,1)}), bf16[128,2,512]{2,0,1:T(8,128)(2,1)S(1)}, u32[]{:S(2)}, u32[]{:S(2)}) async-start(bf16[128,2,512]{2,0,1:T(8,128)(2,1)} %bitcast.548), calls=%async_computation | async-start | bytes 524288 | tf_op jit(solution)/shard_map/all_to_all | solution.py:63
  5.8 5.4 copy-start.4
  11.2 8.6 %all-to-all-start.1 = ((bf16[128,2,512]{2,0,1:T(8,128)(2,1)}), bf16[128,2,512]{2,0,1:T(8,128)(2,1)S(1)}, u32[]{:S(2)}, u32[]{:S(2)}) async-start(bf16[128,2,512]{2,0,1:T(8,128)(2,1)} %bitcast.547), calls=%async_computation.1 | async-start | bytes 524288 | tf_op jit(solution)/shard_map/all_to_all | solution.py:64
  19.9 26.1 %collective-permute-start = (bf16[256,1024]{1,0:T(8,128)(2,1)S(1)}, bf16[256,1024]{1,0:T(8,128)(2,1)S(1)}, u32[]{:S(2)}, u32[]{:S(2)}) collective-permute-start(bf16[256,1024]{1,0:T(8,128)(2,1)S(1)} %pad_maximum_fusion), channel_id=1, source_target_pairs={{0,2},{2,4},{4,6},{6,8},{8,10},{10,12},{12,14},{14,16},{16,18},{18... | collective-permute-start | bytes 1572872 | tf_op jit(solution)/shard_map/ppermute | solution.py:16
  21.8 33.6 %collective-permute-start.1 = (bf16[256,1024]{1,0:T(8,128)(2,1)S(1)}, bf16[256,1024]{1,0:T(8,128)(2,1)S(1)}, u32[]{:S(2)}, u32[]{:S(2)}) collective-permute-start(bf16[256,1024]{1,0:T(8,128)(2,1)S(1)} %pad_maximum_fusion), channel_id=1, source_target_pairs={{0,4},{2,6},{4,8},{6,10},{8,12},{10,14},{12,16},{14,18},{16,20},{1... | collective-permute-start | bytes 1572872 | tf_op jit(solution)/shard_map/ppermute | solution.py:16
  25.3 88.0 %collective-permute-start.5 = (bf16[256,1024]{1,0:T(8,128)(2,1)S(1)}, bf16[256,1024]{1,0:T(8,128)(2,1)S(1)}, u32[]{:S(2)}, u32[]{:S(2)}) collective-permute-start(bf16[256,1024]{1,0:T(8,128)(2,1)S(1)} %pad_maximum_fusion), channel_id=1, source_target_pairs={{0,12},{2,14},{4,16},{6,18},{8,20},{10,22},{12,24},{14,26},{16,28}... | collective-permute-start | bytes 1572872 | tf_op jit(solution)/shard_map/ppermute | solution.py:16
  26.6 85.8 %collective-permute-start.4 = (bf16[256,1024]{1,0:T(8,128)(2,1)S(1)}, bf16[256,1024]{1,0:T(8,128)(2,1)S(1)}, u32[]{:S(2)}, u32[]{:S(2)}) collective-permute-start(bf16[256,1024]{1,0:T(8,128)(2,1)S(1)} %pad_maximum_fusion), channel_id=1, source_target_pairs={{0,10},{2,12},{4,14},{6,16},{8,18},{10,20},{12,22},{14,24},{16,26}... | collective-permute-start | bytes 1572872 | tf_op jit(solution)/shard_map/ppermute | solution.py:16
  28.5 77.9 %collective-permute-start.2 = (bf16[256,1024]{1,0:T(8,128)(2,1)S(1)}, bf16[256,1024]{1,0:T(8,128)(2,1)S(1)}, u32[]{:S(2)}, u32[]{:S(2)}) collective-permute-start(bf16[256,1024]{1,0:T(8,128)(2,1)S(1)} %pad_maximum_fusion), channel_id=1, source_target_pairs={{0,6},{2,8},{4,10},{6,12},{8,14},{10,16},{12,18},{14,20},{16,22},{... | collective-permute-start | bytes 1572872 | tf_op jit(solution)/shard_map/ppermute | solution.py:16
  46.0 65.6 %collective-permute-start.3 = (bf16[256,1024]{1,0:T(8,128)(2,1)S(1)}, bf16[256,1024]{1,0:T(8,128)(2,1)S(1)}, u32[]{:S(2)}, u32[]{:S(2)}) collective-permute-start(bf16[256,1024]{1,0:T(8,128)(2,1)S(1)} %pad_maximum_fusion), channel_id=1, source_target_pairs={{0,8},{2,10},{4,12},{6,14},{8,16},{10,18},{12,20},{14,22},{16,24},... | collective-permute-start | bytes 1572872 | tf_op jit(solution)/shard_map/ppermute | solution.py:16
  55.4 58.7 %collective-permute-start.6 = (bf16[256,1024]{1,0:T(8,128)(2,1)S(1)}, bf16[256,1024]{1,0:T(8,128)(2,1)S(1)}, u32[]{:S(2)}, u32[]{:S(2)}) collective-permute-start(bf16[256,1024]{1,0:T(8,128)(2,1)S(1)} %pad_maximum_fusion), channel_id=1, source_target_pairs={{0,14},{2,16},{4,18},{6,20},{8,22},{10,24},{12,26},{14,28},{16,30}... | collective-permute-start | bytes 1572872 | tf_op jit(solution)/shard_map/ppermute | solution.py:16
  107.2 7.7 %copy-start.5 = (s32[8]{0:T(128)S(1)}, s32[8]{0:T(128)}, u32[]{:S(2)}) copy-start(s32[8]{0:T(128)} %copy-done.4) | copy-start | bytes 100
  427.6 43.3 %collective-permute-start.7 = (bf16[256,1024]{1,0:T(8,128)(2,1)S(1)}, bf16[256,1024]{1,0:T(8,128)(2,1)S(1)}, u32[]{:S(2)}, u32[]{:S(2)}) collective-permute-start(bf16[256,1024]{1,0:T(8,128)(2,1)S(1)} %get-tuple-element.2562), channel_id=1, source_target_pairs={{2,0},{4,2},{6,4},{8,6},{10,8},{12,10},{14,12},{16,14},{18,16},{20... | collective-permute-start | bytes 1572872 | tf_op jit(solution)/shard_map/ppermute | solution.py:16
  429.6 43.3 %collective-permute-start.13 = (bf16[256,1024]{1,0:T(8,128)(2,1)S(1)}, bf16[256,1024]{1,0:T(8,128)(2,1)S(1)}, u32[]{:S(2)}, u32[]{:S(2)}) collective-permute-start(bf16[256,1024]{1,0:T(8,128)(2,1)S(1)} %get-tuple-element.2563), channel_id=1, source_target_pairs={{14,0},{16,2},{18,4},{20,6},{22,8},{24,10},{26,12},{28,14},{30,16}... | collective-permute-start | bytes 1572872 | tf_op jit(solution)/shard_map/ppermute | solution.py:16
  430.9 189.3 %collective-permute-start.12 = (bf16[256,1024]{1,0:T(8,128)(2,1)S(1)}, bf16[256,1024]{1,0:T(8,128)(2,1)S(1)}, u32[]{:S(2)}, u32[]{:S(2)}) collective-permute-start(bf16[256,1024]{1,0:T(8,128)(2,1)S(1)} %get-tuple-element.2564), channel_id=1, source_target_pairs={{12,0},{14,2},{16,4},{18,6},{20,8},{22,10},{24,12},{26,14},{28,16}... | collective-permute-start | bytes 1572872 | tf_op jit(solution)/shard_map/ppermute | solution.py:16
  432.2 207.1 %collective-permute-start.11 = (bf16[256,1024]{1,0:T(8,128)(2,1)S(1)}, bf16[256,1024]{1,0:T(8,128)(2,1)S(1)}, u32[]{:S(2)}, u32[]{:S(2)}) collective-permute-start(bf16[256,1024]{1,0:T(8,128)(2,1)S(1)} %get-tuple-element.2565), channel_id=1, source_target_pairs={{10,0},{12,2},{14,4},{16,6},{18,8},{20,10},{22,12},{24,14},{26,16}... | collective-permute-start | bytes 1572872 | tf_op jit(solution)/shard_map/ppermute | solution.py:16
  434.2 216.5 %collective-permute-start.10 = (bf16[256,1024]{1,0:T(8,128)(2,1)S(1)}, bf16[256,1024]{1,0:T(8,128)(2,1)S(1)}, u32[]{:S(2)}, u32[]{:S(2)}) collective-permute-start(bf16[256,1024]{1,0:T(8,128)(2,1)S(1)} %get-tuple-element.2566), channel_id=1, source_target_pairs={{8,0},{10,2},{12,4},{14,6},{16,8},{18,10},{20,12},{22,14},{24,16},... | collective-permute-start | bytes 1572872 | tf_op jit(solution)/shard_map/ppermute | solution.py:16
  470.9 179.8 %collective-permute-start.9 = (bf16[256,1024]{1,0:T(8,128)(2,1)S(1)}, bf16[256,1024]{1,0:T(8,128)(2,1)S(1)}, u32[]{:S(2)}, u32[]{:S(2)}) collective-permute-start(bf16[256,1024]{1,0:T(8,128)(2,1)S(1)} %get-tuple-element.2567), channel_id=1, source_target_pairs={{6,0},{8,2},{10,4},{12,6},{14,8},{16,10},{18,12},{20,14},{22,16},{... | collective-permute-start | bytes 1572872 | tf_op jit(solution)/shard_map/ppermute | solution.py:16
  472.9 177.8 %collective-permute-start.8 = (bf16[256,1024]{1,0:T(8,128)(2,1)S(1)}, bf16[256,1024]{1,0:T(8,128)(2,1)S(1)}, u32[]{:S(2)}, u32[]{:S(2)}) collective-permute-start(bf16[256,1024]{1,0:T(8,128)(2,1)S(1)} %get-tuple-element.2568), channel_id=1, source_target_pairs={{4,0},{6,2},{8,4},{10,6},{12,8},{14,10},{16,12},{18,14},{20,16},{2... | collective-permute-start | bytes 1572872 | tf_op jit(solution)/shard_map/ppermute | solution.py:16
  661.1 12.6 %all-to-all-start.3 = ((bf16[2,128,512]{2,1,0:T(8,128)(2,1)}), bf16[2,128,512]{2,1,0:T(8,128)(2,1)S(1)}, u32[]{:S(2)}, u32[]{:S(2)}) async-start(bf16[2,128,512]{2,1,0:T(8,128)(2,1)} %bitcast.40), calls=%async_computation.3 | async-start | bytes 524288 | tf_op jit(solution)/shard_map/all_to_all | solution.py:171
where the time goes:
time: 685 us; the launch traced here: 675 us
  starting transfers between devices  186 us (27%)
  matrix products  165 us (24%)
  local copies, waits for them, and re-layouts  143 us (21%)
  waiting for transfers between devices  139 us (20%)
  other arithmetic  19.8 us (3%)
  loops' own time  10.2 us (1%)
  blocking collectives  7.55 us (1%)
    ppermute x14, starting transfers between devices, shifted(): lax.ppermute(value, axis, [(source, source + steps) for source in range(l...  176 us
    ppermute x14, waiting for transfers between devices, shifted(): lax.ppermute(value, axis, [(source, source + steps) for source in range(l...  136 us
    while x16, local copies, waits for them, and re-layouts  63.4 us
    dot_general x16, matrix products, attend_block(): jnp.einsum('htk,thd->kd', grad_scores, block_q, preferred_element_type=jn...  37.3 us
    dot_general x16, matrix products, attend_block(): jnp.einsum('htk,thd->kd', weights_low, block_g, preferred_element_type=jn...  37.1 us
    dot_general x16, matrix products, attend_block(): jnp.einsum('thd,kd->htk', block_g, value_block, preferred_element_type=jn...  24.7 us
    dot_general x16, matrix products, attend_block(): jnp.einsum('htk,kd->thd', weights_low, value_block, preferred_element_typ...  23.3 us
    dot_general x16, matrix products, attend_block(): jnp.einsum('thd,kd->htk', block_q, key_block, preferred_element_type=jnp....  22.3 us
  transfers between devices with their start and end apart: 17, of which 9 were waited for; matrix products, arithmetic and copies ran while one was open for 3% of the time, Pallas kernels for 0%

commit v1 on v0

v1 whole, which is shorter than its diff:
```python
import functools
import math

import jax
import jax.numpy as jnp
from jax import lax
from jax.experimental import pallas as pl
from jax.experimental.pallas import tpu as pltpu
from jax.sharding import PartitionSpec as P

HEAD_SIZE = 128
WINDOW = 8
SCORE_SCALE = 1.0 / math.sqrt(HEAD_SIZE)
LOG2E = math.log2(math.e)
MASKED = -1e30

NT = (((1,), (1,)), ((), ()))
NN = (((1,), (0,)), ((), ()))


def dot(a, b, dims=NN):
    return lax.dot_general(a, b, dims, preferred_element_type=jnp.float32)


def attend_window(slots, heads, info, q_ref, g_ref, kv_ref, low_ref, out_ref, dq_ref, dkv_ref, scratch):
    k_win, v_win, bias, dk_acc, dv_acc = scratch
    rows = q_ref.shape[0]
    keys = slots * rows
    own = info[0]
    for slot in range(slots):
        shard = jnp.maximum(own - (slots - 1) + slot, 0)
        pair = kv_ref[shard]
        k_win[pl.ds(slot * rows, rows), :] = pair[:, :HEAD_SIZE]
        v_win[pl.ds(slot * rows, rows), :HEAD_SIZE] = pair[:, HEAD_SIZE:]
    v_win[pl.ds(0, keys), HEAD_SIZE:] = jnp.ones((keys, HEAD_SIZE), jnp.bfloat16)

    first = own * rows
    query_pos = first + lax.broadcasted_iota(jnp.int32, (rows, HEAD_SIZE), 0)
    low = low_ref[...]
    for block in range(keys // HEAD_SIZE):
        key_pos = (
            first + rows - keys + block * HEAD_SIZE
            + lax.broadcasted_iota(jnp.int32, (rows, HEAD_SIZE), 1)
        )
        allowed = (key_pos >= low) & (key_pos <= query_pos)
        bias[:, pl.ds(block * HEAD_SIZE, HEAD_SIZE)] = jnp.where(allowed, 0.0, MASKED)
    dk_acc[:, pl.ds(0, keys)] = jnp.zeros((HEAD_SIZE, keys), jnp.float32)
    dv_acc[:, pl.ds(0, keys)] = jnp.zeros((HEAD_SIZE, keys), jnp.float32)

    def one_head(head, carry):
        column = pl.multiple_of(head * HEAD_SIZE, HEAD_SIZE)
        query = q_ref[:, pl.ds(column, HEAD_SIZE)]
        grad = g_ref[:, pl.ds(column, HEAD_SIZE)].astype(jnp.float32)
        key_block = k_win[pl.ds(0, keys), :]
        value_block = v_win[pl.ds(0, keys), :]
        scores = dot(query, key_block, NT) * (SCORE_SCALE * LOG2E) + bias[:, pl.ds(0, keys)]
        top = jnp.max(scores, axis=1, keepdims=True)
        weights = jnp.exp2(scores - top).astype(jnp.bfloat16)
        summed = dot(weights, value_block)
        inverse = 1.0 / summed[:, HEAD_SIZE:]
        output = (summed[:, :HEAD_SIZE] * inverse).astype(jnp.bfloat16)
        out_ref[:, pl.ds(column, HEAD_SIZE)] = output
        scaled = (grad * inverse).astype(jnp.bfloat16)
        delta = jnp.sum(output.astype(jnp.float32) * scaled.astype(jnp.float32), axis=1, keepdims=True)
        grad_weights = dot(scaled, value_block[:, :HEAD_SIZE], NT)
        grad_scores = (weights.astype(jnp.float32) * (grad_weights - delta)).astype(jnp.bfloat16)
        dq_ref[:, pl.ds(column, HEAD_SIZE)] = (dot(grad_scores, key_block) * SCORE_SCALE).astype(jnp.bfloat16)
        dk_acc[:, pl.ds(0, keys)] += dot(query.T, grad_scores)
        dv_acc[:, pl.ds(0, keys)] += dot(scaled.T, weights)
        return carry

    lax.fori_loop(0, heads, one_head, 0)

    dkv_ref[...] = jnp.zeros_like(dkv_ref)
    for slot in range(slots):
        shard = own - (slots - 1) + slot
        span = pl.ds(slot * rows, rows)

        @pl.when(shard >= 0)
        def _():
            dkv_ref[shard, :, :HEAD_SIZE] = (dk_acc[:, span] * SCORE_SCALE).T.astype(jnp.bfloat16)
            dkv_ref[shard, :, HEAD_SIZE:] = dv_acc[:, span].T.astype(jnp.bfloat16)


def group_kernel(heads, aliased, info, q_ref, g_ref, kv_ref, low_ref, *rest):
    out_ref, dq_ref, dkv_ref, *scratch = rest[aliased:]
    needed = info[1]
    sizes = (2, 4, WINDOW)
    for place, slots in enumerate(sizes):
        least = sizes[place - 1] if place else 0

        @pl.when((needed > least) & (needed <= slots))
        def _(slots=slots):
            attend_window(
                slots, heads, info, q_ref, g_ref, kv_ref, low_ref, out_ref, dq_ref, dkv_ref, scratch
            )


def attend_group(group, groups, info, queries, gradient, kv_all, low, buffers):
    rows, width = queries.shape
    columns = width // groups
    heads = columns // HEAD_SIZE
    keys = WINDOW * rows
    whole = lambda shape: pl.BlockSpec(shape, lambda i, info: (0,) * len(shape))
    block = pl.BlockSpec((rows, columns), lambda i, info: (0, group))
    aliased = len(buffers)
    flops = 6 * 2 * heads * rows * keys * HEAD_SIZE
    return pl.pallas_call(
        functools.partial(group_kernel, heads, aliased),
        grid_spec=pltpu.PrefetchScalarGridSpec(
            num_scalar_prefetch=1,
            grid=(1,),
            in_specs=[block, block, whole(kv_all.shape), whole(low.shape)]
            + [pl.BlockSpec(memory_space=pl.ANY)] * aliased,
            out_specs=[block, block, whole(kv_all.shape)],
            scratch_shapes=[
                pltpu.VMEM((keys, HEAD_SIZE), jnp.bfloat16),
                pltpu.VMEM((keys, 2 * HEAD_SIZE), jnp.bfloat16),
                pltpu.VMEM((rows, keys), jnp.float32),
                pltpu.VMEM((HEAD_SIZE, keys), jnp.float32),
                pltpu.VMEM((HEAD_SIZE, keys), jnp.float32),
            ],
        ),
        out_shape=[
            jax.ShapeDtypeStruct(queries.shape, jnp.bfloat16),
            jax.ShapeDtypeStruct(queries.shape, jnp.bfloat16),
            jax.ShapeDtypeStruct(kv_all.shape, jnp.bfloat16),
        ],
        input_output_aliases={5 + place: place for place in range(aliased)},
        compiler_params=pltpu.CompilerParams(vmem_limit_bytes=56 * 1024 * 1024),
        cost_estimate=pl.CostEstimate(
            flops=flops, bytes_accessed=4 * rows * columns * 2 + 4 * kv_all.size, transcendentals=heads * rows * keys
        ),
        name=f"attend_group_{group}",
    )(info, queries, gradient, kv_all, low, *buffers)


def body(queries, key_vectors, value_vectors, output_gradient, doc_lengths):
    own = lax.axis_index("ctx")
    rows = queries.shape[0]
    local = key_vectors.shape[0]
    all_groups = key_vectors.shape[1] // HEAD_SIZE
    pairs = jnp.concatenate(
        [
            key_vectors.reshape(local, all_groups, HEAD_SIZE),
            value_vectors.reshape(local, all_groups, HEAD_SIZE),
        ],
        axis=2,
    )
    pairs = lax.all_to_all(pairs, "tp", split_axis=1, concat_axis=0, tiled=True)
    groups = pairs.shape[1]

    doc_starts = jnp.cumsum(doc_lengths, dtype=jnp.int32) - doc_lengths
    first = own * rows
    query_pos = first + jnp.arange(rows, dtype=jnp.int32)
    low = jnp.max(jnp.where(doc_starts[None, :] <= query_pos[:, None], doc_starts[None, :], 0), axis=1)
    needed = jnp.clip(own - low[0] // rows + 1, 1, WINDOW)
    info = jnp.stack([own, needed]).astype(jnp.int32)
    low = jnp.broadcast_to(low[:, None], (rows, HEAD_SIZE))

    gathered = [lax.all_gather(pairs[:, group], "ctx", axis=0) for group in range(groups)]
    buffers = ()
    owned = []
    for group in range(groups):
        *buffers, partial_grads = attend_group(
            group, groups, info, queries, output_gradient, gathered[group], low, buffers
        )
        owned.append(lax.psum_scatter(partial_grads, "ctx", scatter_dimension=0, tiled=False))
    out, dq = buffers
    grads = jnp.stack(owned, axis=1)
    grads = lax.all_to_all(grads, "tp", split_axis=0, concat_axis=1, tiled=True)
    dk = grads[:, :, :HEAD_SIZE].reshape(local, all_groups * HEAD_SIZE)
    dv = grads[:, :, HEAD_SIZE:].reshape(local, all_groups * HEAD_SIZE)
    return out, dq, dk, dv


def solution(mesh):
    tokens = P(("ctx", "tp"), None)
    heads = P("ctx", "tp")
    return jax.shard_map(
        body,
        mesh=mesh,
        in_specs=(heads, tokens, tokens, heads, P()),
        out_specs=(heads, heads, tokens, tokens),
        check_vma=False,
    )
```

time: 685 us -> 491 us (0.72)
  waiting for transfers between devices: 139 us -> 393 us
  starting transfers between devices: 186 us -> 0.31 us
  matrix products: 165 us -> 0 us
  local copies, waits for them, and re-layouts: 143 us -> 7.25 us
  Pallas kernels: 0 us -> 48.2 us
  other arithmetic: 19.8 us -> 2.08 us
  between operations: 4.01 us -> 16.8 us
  blocking collectives: 7.55 us -> 19.8 us
  loops' own time: 10.2 us -> 0 us
    reduce_scatter x0 -> x4, waiting for transfers between devices: none -> 265 us  [body(): lax.psum_scatter(partial_grads, 'ctx', scatter_dimension=0, tiled=False)]
    ppermute x14 -> x0, starting transfers between devices: 176 us -> none  [shifted(): lax.ppermute(value, axis, [(source, source + steps) for source in range(l...]
    dot_general x96 -> x0, matrix products: 165 us -> none  [the longest x16 37.3 us: attend_block(): jnp.einsum('htk,thd->kd', grad_scores, block_q, preferred_element_type=jn...]
    ppermute x14 -> x0, waiting for transfers between devices: 136 us -> none  [shifted(): lax.ppermute(value, axis, [(source, source + steps) for source in range(l...]
    all_gather x0 -> x4, waiting for transfers between devices: none -> 124 us  [body(): lax.all_gather(pairs[:, group], 'ctx', axis=0)]
    while x16 -> x0, local copies, waits for them, and re-layouts: 63.4 us -> none
    pallas_call x0 -> x4, Pallas kernels: none -> 48.2 us  [attend_group(): pl.pallas_call(functools.partial(group_kernel, heads, aliased), grid_spec...]
    dynamic_slice x64 -> x0, local copies, waits for them, and re-layouts: 32.5 us -> none  [the longest x32 16.3 us: one_block(): lax.dynamic_slice_in_dim(q_set, column, head_block * HEAD_SIZE, 1)]
  transfers between devices with their start and end apart: 17 -> 8, of which waited for: 9 -> 8; matrix products, arithmetic and copies ran while one was open for 3% -> 0% of each run, Pallas kernels for 0% -> 7%
where the time goes in v1:
time: 491 us; the launch traced here: 487 us
  waiting for transfers between devices  393 us (80%)
  Pallas kernels  48.2 us (10%)
  blocking collectives  19.8 us (4%)
  between operations  16.8 us (3%)
  local copies, waits for them, and re-layouts  7.25 us (1%)
    reduce_scatter x4, waiting for transfers between devices, body(): lax.psum_scatter(partial_grads, 'ctx', scatter_dimension=0, tiled=False)  265 us
    all_gather x4, waiting for transfers between devices, body(): lax.all_gather(pairs[:, group], 'ctx', axis=0)  124 us
    pallas_call x4, Pallas kernels, attend_group(): pl.pallas_call(functools.partial(group_kernel, heads, aliased), grid_spec...  48.2 us
    all_to_all x1, blocking collectives, body(): pairs = lax.all_to_all(pairs, 'tp', split_axis=1, concat_axis=0, tiled=True)  10.7 us
  transfers between devices with their start and end apart: 8, of which 8 were waited for; matrix products, arithmetic and copies ran while one was open for 0% of the time, Pallas kernels for 7%

profile of v1, /device:TPU:18, one launch (start us, length us, event | category | flops | bytes accessed | tf_op | source)
XLA Modules:
  0.0 487.2 jit_solution(13815315075515170316)
XLA Ops:
  7.2 0.0 all-gather.15.cloned.1.call-start
  7.2 1.1 copy.41
  8.3 1.1 copy.42
  9.5 0.2 copy.43
  9.7 0.0 copy-start
  9.7 10.7 %all_to_all.36 = bf16[128,8,256]{2,0,1:T(8,128)(2,1)S(1)} all-to-all(bf16[128,8,256]{2,0,1:T(8,128)(2,1)S(1)} %copy.43), channel_id=1, replica_groups=mesh['ctx'=16,'tp'=2] {'tp'}, dimensions={1} | all-to-all | bytes 1048576 | tf_op jit(solution)/shard_map/all_to_all | solution.py:150
  20.4 0.8 fusion.1
  21.2 0.0 all-gather.15.cloned.1.call-update
  21.3 0.0 all-gather.13.cloned.1.call-start
  21.3 0.7 all-gather.13.cloned.1.call-update
  22.0 0.0 all-gather.11.cloned.1.call-start
  22.1 0.7 all-gather.11.cloned.1.call-update
  22.7 0.0 all-gather.9.cloned.1.call-start
  22.8 0.5 all-gather.9.cloned.1.call-update
  23.3 0.0 reduce-scatter.11.cloned.1.call-start
  23.4 0.2 reduce-window.9
  23.6 0.1 select_reduce_fusion
  23.7 0.5 slice.21
  26.8 0.6 pad_add_fusion.info
  27.4 32.9 %all-gather.15.cloned.1.call-done = bf16[4096,1,256]{2,0,1:T(8,128)(2,1)} async-done(((bf16[256,1,256]{2,0,1:T(8,128)(2,1)}), bf16[4096,1,256]{2,0,1:T(8,128)(2,1)}) %all-gather.15.cloned.1.call-update) | async-done | bytes 2097168 | tf_op jit(solution)/shard_map/all_gather | solution.py:161
  60.2 0.8 broadcast_in_dim.13.low_ref
  61.0 11.9 %attend_group_0.1 = (bf16[256,4096]{1,0:T(8,128)(2,1)}, bf16[256,4096]{1,0:T(8,128)(2,1)}, bf16[16,256,256]{2,1,0:T(8,128)(2,1)}) custom-call(s32[2]{0:T(128)} %pad_add_fusion.info, bf16[256,4096]{1,0:T(8,128)(2,1)} %q_ref.7, bf16[256,4096]{1,0:T(8,128)(2,1)} %g_ref.7, bf16[16,256,256]{2,1,0:T(8,128)(2,1)} %bitcast.38, s32[256,128]{1,0:T(8,128)} %broadcast_in_dim.13.low_ref), custom_call_target="tpu_custom_call" | custom-call | flops 6442450944 | bytes 6291456 | tf_op jit(solution)/shard_map/attend_group_0/pallas_call | solution.py:108
  72.9 30.2 %all-gather.13.cloned.1.call-done = bf16[4096,1,256]{2,0,1:T(8,128)(2,1)} async-done(((bf16[256,1,256]{2,0,1:T(8,128)(2,1)}), bf16[4096,1,256]{2,0,1:T(8,128)(2,1)}) %all-gather.13.cloned.1.call-update) | async-done | bytes 2097168 | tf_op jit(solution)/shard_map/all_gather | solution.py:161
  103.1 12.1 %attend_group_1.1 = (bf16[256,4096]{1,0:T(8,128)(2,1)}, bf16[256,4096]{1,0:T(8,128)(2,1)}, bf16[16,256,256]{2,1,0:T(8,128)(2,1)}) custom-call(s32[2]{0:T(128)} %pad_add_fusion.info, bf16[256,4096]{1,0:T(8,128)(2,1)} %q_ref.7, bf16[256,4096]{1,0:T(8,128)(2,1)} %g_ref.7, bf16[16,256,256]{2,1,0:T(8,128)(2,1)} %bitcast.41, ...), custom_call_target="tpu_custom_call", output_to_operand_aliasing={{0}: (5, {}), {1}: (6, {})} | custom-call | flops 6442450944 | bytes 6291456 | tf_op jit(solution)/shard_map/attend_group_1/pallas_call | solution.py:108
  115.2 30.3 %all-gather.11.cloned.1.call-done = bf16[4096,1,256]{2,0,1:T(8,128)(2,1)} async-done(((bf16[256,1,256]{2,0,1:T(8,128)(2,1)}), bf16[4096,1,256]{2,0,1:T(8,128)(2,1)}) %all-gather.11.cloned.1.call-update) | async-done | bytes 2097168 | tf_op jit(solution)/shard_map/all_gather | solution.py:161
  145.5 11.9 %attend_group_2.1 = (bf16[256,4096]{1,0:T(8,128)(2,1)}, bf16[256,4096]{1,0:T(8,128)(2,1)}, bf16[16,256,256]{2,1,0:T(8,128)(2,1)}) custom-call(s32[2]{0:T(128)} %pad_add_fusion.info, bf16[256,4096]{1,0:T(8,128)(2,1)} %q_ref.7, bf16[256,4096]{1,0:T(8,128)(2,1)} %g_ref.7, bf16[16,256,256]{2,1,0:T(8,128)(2,1)} %bitcast.39, ...), custom_call_target="tpu_custom_call", output_to_operand_aliasing={{0}: (5, {}), {1}: (6, {})} | custom-call | flops 6442450944 | bytes 6291456 | tf_op jit(solution)/shard_map/attend_group_2/pallas_call | solution.py:108
  157.5 30.3 %all-gather.9.cloned.1.call-done = bf16[4096,1,256]{2,0,1:T(8,128)(2,1)} async-done(((bf16[256,1,256]{2,0,1:T(8,128)(2,1)}), bf16[4096,1,256]{2,0,1:T(8,128)(2,1)}) %all-gather.9.cloned.1.call-update) | async-done | bytes 2097168 | tf_op jit(solution)/shard_map/all_gather | solution.py:161
  187.7 12.3 %attend_group_3.1 = (bf16[256,4096]{1,0:T(8,128)(2,1)}, bf16[256,4096]{1,0:T(8,128)(2,1)}, bf16[16,256,256]{2,1,0:T(8,128)(2,1)}) custom-call(s32[2]{0:T(128)} %pad_add_fusion.info, bf16[256,4096]{1,0:T(8,128)(2,1)} %q_ref.7, bf16[256,4096]{1,0:T(8,128)(2,1)} %g_ref.7, bf16[16,256,256]{2,1,0:T(8,128)(2,1)} %bitcast.40, ...), custom_call_target="tpu_custom_call", output_to_operand_aliasing={{0}: (5, {}), {1}: (6, {})} | custom-call | flops 6442450944 | bytes 6291456 | tf_op jit(solution)/shard_map/attend_group_3/pallas_call | solution.py:108
  200.0 0.0 reduce-scatter.11.cloned.1.call-update
  200.0 0.0 reduce-scatter.9.cloned.1.call-start
  200.1 0.5 reduce-scatter.9.cloned.1.call-update
  200.6 0.0 reduce-scatter.7.cloned.1.call-start
  200.6 0.7 reduce-scatter.7.cloned.1.call-update
  201.4 0.0 reduce-scatter.5.cloned.1.call-start
  201.4 0.7 reduce-scatter.5.cloned.1.call-update
  202.1 71.5 %reduce-scatter.11.cloned.1.call-done = bf16[1,256,256]{2,1,0:T(8,128)(2,1)} async-done(((bf16[16,256,256]{2,1,0:T(8,128)(2,1)}), bf16[1,256,256]{2,1,0:T(8,128)(2,1)}) %reduce-scatter.11.cloned.1.call-update) | async-done | bytes 131088 | tf_op jit(solution)/shard_map/reduce_scatter | solution.py:168
  273.6 64.6 %reduce-scatter.9.cloned.1.call-done = bf16[1,256,256]{2,1,0:T(8,128)(2,1)} async-done(((bf16[16,256,256]{2,1,0:T(8,128)(2,1)}), bf16[1,256,256]{2,1,0:T(8,128)(2,1)}) %reduce-scatter.9.cloned.1.call-update) | async-done | bytes 131088 | tf_op jit(solution)/shard_map/reduce_scatter | solution.py:168
  338.2 64.4 %reduce-scatter.7.cloned.1.call-done = bf16[1,256,256]{2,1,0:T(8,128)(2,1)} async-done(((bf16[16,256,256]{2,1,0:T(8,128)(2,1)}), bf16[1,256,256]{2,1,0:T(8,128)(2,1)}) %reduce-scatter.7.cloned.1.call-update) | async-done | bytes 131088 | tf_op jit(solution)/shard_map/reduce_scatter | solution.py:168
  402.6 64.8 %reduce-scatter.5.cloned.1.call-done = bf16[1,256,256]{2,1,0:T(8,128)(2,1)} async-done(((bf16[16,256,256]{2,1,0:T(8,128)(2,1)}), bf16[1,256,256]{2,1,0:T(8,128)(2,1)}) %reduce-scatter.5.cloned.1.call-update) | async-done | bytes 131088 | tf_op jit(solution)/shard_map/reduce_scatter | solution.py:168
  467.4 1.2 pad_maximum_fusion.1
  468.5 0.4 copy.45
  469.0 9.1 %all_to_all.37 = bf16[256,4,256]{2,1,0:T(4,128)(2,1)S(1)} all-to-all(bf16[256,4,256]{2,1,0:T(4,128)(2,1)S(1)} %copy.45), channel_id=1, replica_groups=mesh['ctx'=16,'tp'=2] {'tp'}, dimensions={0} | all-to-all | bytes 1048576 | tf_op jit(solution)/shard_map/all_to_all | solution.py:171
  478.1 0.1 copy.46
  478.2 0.1 fusion
  478.3 0.2 copy.49
  478.5 0.9 copy.51
  479.4 0.2 copy.48
  479.5 0.9 copy.50
  (6 shorter events, 0.1 us)
Async XLA Ops:
  7.2 53.1 %all-gather.15.cloned.1.call-start = ((), (), s32[]{:S(2)}) async-start(), calls=%async_computation.13 | async-start | bytes 2228224 | tf_op jit(solution)/shard_map/all_gather | solution.py:161
  9.7 13.6 %copy-start = (s32[8]{0:T(128)S(1)}, s32[8]{0:T(128)}, u32[]{:S(2)}) copy-start(s32[8]{0:T(128)} %param.9) | copy-start | bytes 100
  21.3 81.9 %all-gather.13.cloned.1.call-start = ((), (), s32[]{:S(2)}) async-start(), calls=%async_computation.12 | async-start | bytes 2228224 | tf_op jit(solution)/shard_map/all_gather | solution.py:161
  22.0 123.5 %all-gather.11.cloned.1.call-start = ((), (), s32[]{:S(2)}) async-start(), calls=%async_computation.11 | async-start | bytes 2228224 | tf_op jit(solution)/shard_map/all_gather | solution.py:161
  22.7 165.0 %all-gather.9.cloned.1.call-start = ((), (), s32[]{:S(2)}) async-start(), calls=%async_computation.10 | async-start | bytes 2228224 | tf_op jit(solution)/shard_map/all_gather | solution.py:161
  23.3 250.2 %reduce-scatter.11.cloned.1.call-start = ((), (), s32[]{:S(2)}) async-start(), calls=%async_computation.9 | async-start | bytes 2228224 | tf_op jit(solution)/shard_map/reduce_scatter | solution.py:168
  200.0 138.2 %reduce-scatter.9.cloned.1.call-start = ((), (), s32[]{:S(2)}) async-start(), calls=%async_computation.8 | async-start | bytes 2228224 | tf_op jit(solution)/shard_map/reduce_scatter | solution.py:168
  200.6 202.0 %reduce-scatter.7.cloned.1.call-start = ((), (), s32[]{:S(2)}) async-start(), calls=%async_computation.7 | async-start | bytes 2228224 | tf_op jit(solution)/shard_map/reduce_scatter | solution.py:168
  201.4 266.0 %reduce-scatter.5.cloned.1.call-start = ((), (), s32[]{:S(2)}) async-start(), calls=%async_computation.6 | async-start | bytes 2228224 | tf_op jit(solution)/shard_map/reduce_scatter | solution.py:168
Sparse Core Ops, SparseCore 0:
  21.4 38.8 all-gather.14
  63.0 40.1 all-gather.12
  105.3 40.1 all-gather.10
  147.5 40.1 all-gather.8
  200.1 73.3 reduce-scatter.10
  277.6 60.5 reduce-scatter.8
  341.9 60.6 reduce-scatter.6
  406.8 60.5 reduce-scatter.4

commit v2 on v1

v2 whole, which is shorter than its diff:
```python
import functools
import math

import jax
import jax.numpy as jnp
from jax import lax
from jax.experimental import pallas as pl
from jax.experimental.pallas import tpu as pltpu
from jax.sharding import PartitionSpec as P

HEAD_SIZE = 128
WINDOW = 8
CHUNKS = 2
SCORE_SCALE = 1.0 / math.sqrt(HEAD_SIZE)
LOG2E = math.log2(math.e)
MASKED = -1e30

NT = (((1,), (1,)), ((), ()))
NN = (((1,), (0,)), ((), ()))


def dot(a, b, dims=NN):
    return lax.dot_general(a, b, dims, preferred_element_type=jnp.float32)


def attend_window(slots, heads, own, q_ref, g_ref, window_refs, low_ref, out_ref, dq_ref, even_ref, odd_ref, scratch):
    k_win, v_win, bias, dk_acc, dv_acc = scratch
    rows = q_ref.shape[0]
    keys = slots * rows
    for slot in range(slots):
        pair = window_refs[slots - 1 - slot][...]
        k_win[pl.ds(slot * rows, rows), :] = pair[:, :HEAD_SIZE]
        v_win[pl.ds(slot * rows, rows), :HEAD_SIZE] = pair[:, HEAD_SIZE:]
    v_win[pl.ds(0, keys), HEAD_SIZE:] = jnp.ones((keys, HEAD_SIZE), jnp.bfloat16)

    first = own * rows
    query_pos = first + lax.broadcasted_iota(jnp.int32, (rows, HEAD_SIZE), 0)
    low = low_ref[...]
    for block in range(keys // HEAD_SIZE):
        key_pos = (
            first + rows - keys + block * HEAD_SIZE
            + lax.broadcasted_iota(jnp.int32, (rows, HEAD_SIZE), 1)
        )
        allowed = (key_pos >= low) & (key_pos <= query_pos)
        bias[:, pl.ds(block * HEAD_SIZE, HEAD_SIZE)] = jnp.where(allowed, 0.0, MASKED)
    dk_acc[:, pl.ds(0, keys)] = jnp.zeros((HEAD_SIZE, keys), jnp.float32)
    dv_acc[:, pl.ds(0, keys)] = jnp.zeros((HEAD_SIZE, keys), jnp.float32)

    def one_head(head, carry):
        column = pl.multiple_of(head * HEAD_SIZE, HEAD_SIZE)
        query = q_ref[:, pl.ds(column, HEAD_SIZE)]
        grad = g_ref[:, pl.ds(column, HEAD_SIZE)].astype(jnp.float32)
        key_block = k_win[pl.ds(0, keys), :]
        value_block = v_win[pl.ds(0, keys), :]
        scores = dot(query, key_block, NT) * (SCORE_SCALE * LOG2E) + bias[:, pl.ds(0, keys)]
        top = jnp.max(scores, axis=1, keepdims=True)
        weights = jnp.exp2(scores - top).astype(jnp.bfloat16)
        summed = dot(weights, value_block)
        inverse = 1.0 / summed[:, HEAD_SIZE:]
        output = (summed[:, :HEAD_SIZE] * inverse).astype(jnp.bfloat16)
        out_ref[:, pl.ds(column, HEAD_SIZE)] = output
        scaled = (grad * inverse).astype(jnp.bfloat16)
        delta = jnp.sum(output.astype(jnp.float32) * scaled.astype(jnp.float32), axis=1, keepdims=True)
        grad_weights = dot(scaled, value_block[:, :HEAD_SIZE], NT)
        grad_scores = (weights.astype(jnp.float32) * (grad_weights - delta)).astype(jnp.bfloat16)
        dq_ref[:, pl.ds(column, HEAD_SIZE)] = (dot(grad_scores, key_block) * SCORE_SCALE).astype(jnp.bfloat16)
        dk_acc[:, pl.ds(0, keys)] += dot(query.T, grad_scores)
        dv_acc[:, pl.ds(0, keys)] += dot(scaled.T, weights)
        return carry

    lax.fori_loop(0, heads, one_head, 0)

    for offset in range(WINDOW):
        target = (odd_ref if offset % 2 else even_ref).at[offset // 2]
        if offset < slots:
            span = pl.ds((slots - 1 - offset) * rows, rows)
            target[:, :HEAD_SIZE] = (dk_acc[:, span] * SCORE_SCALE).T.astype(jnp.bfloat16)
            target[:, HEAD_SIZE:] = dv_acc[:, span].T.astype(jnp.bfloat16)
        else:
            target[...] = jnp.zeros(target.shape, jnp.bfloat16)


def group_kernel(heads, aliased, info, q_ref, g_ref, own_ref, far_ref, x_ref, c_ref, low_ref, *rest):
    out_ref, dq_ref, even_ref, odd_ref, *scratch = rest[aliased:]
    needed = info[1]
    window_refs = [
        own_ref, c_ref.at[0], x_ref.at[0], c_ref.at[1], far_ref, c_ref.at[2], x_ref.at[1], c_ref.at[3]
    ]
    sizes = (2, 4, WINDOW)
    for place, slots in enumerate(sizes):
        least = sizes[place - 1] if place else 0

        @pl.when((needed > least) & (needed <= slots))
        def _(slots=slots):
            attend_window(
                slots, heads, info[0], q_ref, g_ref, window_refs, low_ref,
                out_ref, dq_ref, even_ref, odd_ref, scratch,
            )


def attend_groups(first_group, count, groups, info, queries, gradient, window, low, buffers):
    rows, width = queries.shape
    columns = width // groups
    heads = columns // HEAD_SIZE
    keys = WINDOW * rows
    pair = 2 * HEAD_SIZE
    block = pl.BlockSpec((rows, columns), lambda i, info: (0, first_group + i))
    shard = pl.BlockSpec((rows, pair), lambda i, info: (0, i))
    several = lambda number: pl.BlockSpec((number, rows, pair), lambda i, info: (0, 0, i))
    half = WINDOW // 2
    aliased = len(buffers)
    flops = 6 * 2 * heads * rows * keys * HEAD_SIZE * count
    grads = jax.ShapeDtypeStruct((half, rows, pair * count), jnp.bfloat16)
    return pl.pallas_call(
        functools.partial(group_kernel, heads, aliased),
        grid_spec=pltpu.PrefetchScalarGridSpec(
            num_scalar_prefetch=1,
            grid=(count,),
            in_specs=[block, block, shard, shard, several(half // 2), several(half)]
            + [pl.BlockSpec(low.shape, lambda i, info: (0, 0))]
            + [pl.BlockSpec(memory_space=pl.ANY)] * aliased,
            out_specs=[block, block, several(half), several(half)],
            scratch_shapes=[
                pltpu.VMEM((keys, HEAD_SIZE), jnp.bfloat16),
                pltpu.VMEM((keys, pair), jnp.bfloat16),
                pltpu.VMEM((rows, keys), jnp.float32),
                pltpu.VMEM((HEAD_SIZE, keys), jnp.float32),
                pltpu.VMEM((HEAD_SIZE, keys), jnp.float32),
            ],
        ),
        out_shape=[
            jax.ShapeDtypeStruct(queries.shape, jnp.bfloat16),
            jax.ShapeDtypeStruct(queries.shape, jnp.bfloat16),
            grads,
            grads,
        ],
        input_output_aliases={8 + place: place for place in range(aliased)},
        compiler_params=pltpu.CompilerParams(vmem_limit_bytes=56 * 1024 * 1024),
        cost_estimate=pl.CostEstimate(
            flops=flops,
            bytes_accessed=count * (8 * rows * columns + 8 * keys * HEAD_SIZE),
            transcendentals=count * heads * rows * keys,
        ),
        name=f"attend_groups_{first_group}",
    )(info, queries, gradient, *window, low, *buffers)


def shifted(value, steps):
    count = lax.axis_size("ctx")
    sources = range(max(0, -steps), min(count, count - steps))
    return lax.ppermute(value, "ctx", [(source, source + steps) for source in sources])


def swapped(value, bit):
    return lax.ppermute(value, "ctx", [(place, place ^ bit) for place in range(lax.axis_size("ctx"))])


def tp_exchange(block_for):
    count = lax.axis_size("tp")
    own = lax.axis_index("tp")
    received = [block_for(own)]
    for step in range(1, count):
        sent = block_for(lax.rem(own + step, count))
        received.append(lax.ppermute(sent, "tp", [(place, (place + step) % count) for place in range(count)]))
    return [
        functools.reduce(
            lambda rest, step: jnp.where(lax.rem(own - step + count, count) == place, received[step], rest),
            range(1, count),
            received[0],
        )
        for place in range(count)
    ]


def gather_window(own_pair, own):
    far = shifted(own_pair, WINDOW // 2)
    beyond = shifted(far, WINDOW // 2)
    low_x = (own // 2) % 2 == 0
    low_c = own % 2 == 0
    x_sent = jnp.stack([jnp.where(low_x, own_pair, far), jnp.where(low_x, far, beyond)])
    x_pairs = swapped(x_sent, 2)
    evens = [own_pair, x_pairs[0], far, x_pairs[1], beyond]
    c_sent = jnp.stack([jnp.where(low_c, evens[place], evens[place + 1]) for place in range(WINDOW // 2)])
    c_pairs = swapped(c_sent, 1)
    return own_pair, far, x_pairs, c_pairs


def reduce_window(even, odd, own):
    wide = lambda part: part.astype(jnp.float32)
    low_x = (own // 2) % 2 == 0
    low_c = own % 2 == 0
    got = wide(swapped(odd, 1))
    even = wide(even)
    nothing = jnp.zeros_like(got[0])
    sums = [even[0] + jnp.where(low_c, got[0], nothing)]
    for place in range(1, WINDOW // 2):
        sums.append(even[place] + jnp.where(low_c, got[place], got[place - 1]))
    sums.append(jnp.where(low_c, nothing, got[WINDOW // 2 - 1]))
    got = wide(swapped(jnp.stack([sums[1], sums[3]]).astype(jnp.bfloat16), 2))
    near = sums[0] + jnp.where(low_x, got[0], nothing)
    far = sums[2] + jnp.where(low_x, got[1], got[0])
    beyond = sums[4] + jnp.where(low_x, nothing, got[1])
    far = far + wide(shifted(beyond.astype(jnp.bfloat16), -(WINDOW // 2)))
    near = near + wide(shifted(far.astype(jnp.bfloat16), -(WINDOW // 2)))
    return near.astype(jnp.bfloat16)


def body(queries, key_vectors, value_vectors, output_gradient, doc_lengths):
    own = lax.axis_index("ctx")
    rows = queries.shape[0]
    local = key_vectors.shape[0]
    all_groups = key_vectors.shape[1] // HEAD_SIZE
    groups = all_groups // lax.axis_size("tp")
    pair = 2 * HEAD_SIZE
    columns = groups * HEAD_SIZE

    def pairs_for(place):
        keys = lax.dynamic_slice_in_dim(key_vectors, place * columns, columns, 1)
        values = lax.dynamic_slice_in_dim(value_vectors, place * columns, columns, 1)
        joined = [
            part[:, group * HEAD_SIZE : (group + 1) * HEAD_SIZE] for group in range(groups) for part in (keys, values)
        ]
        return jnp.concatenate(joined, axis=1)

    pairs = jnp.concatenate(tp_exchange(pairs_for), axis=0)

    doc_starts = jnp.cumsum(doc_lengths, dtype=jnp.int32) - doc_lengths
    query_pos = own * rows + jnp.arange(rows, dtype=jnp.int32)
    low = jnp.max(jnp.where(doc_starts[None, :] <= query_pos[:, None], doc_starts[None, :], 0), axis=1)
    needed = jnp.clip(own - low[0] // rows + 1, 1, WINDOW)
    info = jnp.stack([own, needed]).astype(jnp.int32)
    low = jnp.broadcast_to(low[:, None], (rows, HEAD_SIZE))

    count = max(1, groups // CHUNKS)
    starts = range(0, groups, count)
    windows = [gather_window(pairs[:, start * pair : (start + count) * pair], own) for start in starts]
    buffers = ()
    sums = []
    for start, window in zip(starts, windows):
        *buffers, even, odd = attend_groups(
            start, count, groups, info, queries, output_gradient, window, low, buffers
        )
        total = reduce_window(even, odd, own)
        sums.append(
            tp_exchange(lambda place: lax.dynamic_slice_in_dim(total, place * local, local, 0))
        )
    out, dq = buffers

    def output(first):
        parts = [
            sums[group // count][place][:, (group % count) * pair + first :][:, :HEAD_SIZE]
            for place in range(lax.axis_size("tp"))
            for group in range(groups)
        ]
        return jnp.concatenate(parts, axis=1)

    return out, dq, output(0), output(HEAD_SIZE)


def solution(mesh):
    tokens = P(("ctx", "tp"), None)
    heads = P("ctx", "tp")
    return jax.shard_map(
        body,
        mesh=mesh,
        in_specs=(heads, tokens, tokens, heads, P()),
        out_specs=(heads, heads, tokens, tokens),
        check_vma=False,
    )
```

time: 491 us -> 214 us (0.44)
  waiting for transfers between devices: 393 us -> 68.3 us
  starting transfers between devices: 0.31 us -> 61.2 us
  blocking collectives: 19.8 us -> 0 us
  between operations: 16.8 us -> 3.78 us
  other arithmetic: 2.08 us -> 12.7 us
  local copies, waits for them, and re-layouts: 7.25 us -> 13.1 us
  Pallas kernels: 48.2 us -> 53.2 us
    reduce_scatter x4 -> x0, waiting for transfers between devices: 265 us -> none  [body(): lax.psum_scatter(partial_grads, 'ctx', scatter_dimension=0, tiled=False)]
    all_gather x4 -> x0, waiting for transfers between devices: 124 us -> none  [body(): lax.all_gather(pairs[:, group], 'ctx', axis=0)]
    ppermute x0 -> x19, waiting for transfers between devices: none -> 68.3 us  [the longest x8 29.4 us: shifted(): lax.ppermute(value, 'ctx', [(source, source + steps) for source in sources])]
    ppermute x0 -> x19, starting transfers between devices: none -> 61.2 us  [the longest x8 36.4 us: swapped(): lax.ppermute(value, 'ctx', [(place, place ^ bit) for place in range(lax.a...]
    all_to_all x2 -> x0, blocking collectives: 19.8 us -> none  [the longest x1 10.7 us: body(): pairs = lax.all_to_all(pairs, 'tp', split_axis=1, concat_axis=0, tiled=True)]
    convert_element_type x0 -> x12, other arithmetic: none -> 8.95 us  [the longest x6 3.67 us: reduce_window(): wide = lambda part: part.astype(jnp.float32)]
    unnamed x6 -> x47, local copies, waits for them, and re-layouts: 3.95 us -> 10.2 us
    pallas_call x4 -> x2, Pallas kernels: 48.2 us -> 53.2 us  [attend_groups(): pl.pallas_call(functools.partial(group_kernel, heads, aliased), grid_spec...]
  transfers between devices with their start and end apart: 8 -> 19, of which waited for: 8 -> 12; matrix products, arithmetic and copies ran while one was open for 0% -> 6% of each run, Pallas kernels for 7% -> 25%
where the time goes in v2:
time: 214 us; the launch traced here: 212 us
  waiting for transfers between devices  68.3 us (32%)
  starting transfers between devices  61.2 us (29%)
  Pallas kernels  53.2 us (25%)
  local copies, waits for them, and re-layouts  13.1 us (6%)
  other arithmetic  12.7 us (6%)
  between operations  3.78 us (2%)
    pallas_call x2, Pallas kernels, attend_groups(): pl.pallas_call(functools.partial(group_kernel, heads, aliased), grid_spec...  53.2 us
    ppermute x8, starting transfers between devices, swapped(): lax.ppermute(value, 'ctx', [(place, place ^ bit) for place in range(lax.a...  36.4 us
    ppermute x8, waiting for transfers between devices, shifted(): lax.ppermute(value, 'ctx', [(source, source + steps) for source in sources])  29.4 us
    ppermute x8, waiting for transfers between devices, swapped(): lax.ppermute(value, 'ctx', [(place, place ^ bit) for place in range(lax.a...  29.1 us
    ppermute x8, starting transfers between devices, shifted(): lax.ppermute(value, 'ctx', [(source, source + steps) for source in sources])  20 us
    unnamed x47, local copies, waits for them, and re-layouts  10.2 us
    ppermute x3, waiting for transfers between devices, tp_exchange(): lax.ppermute(sent, 'tp', [(place, (place + step) % count) for place in ra...  9.86 us
    ppermute x3, starting transfers between devices, tp_exchange(): lax.ppermute(sent, 'tp', [(place, (place + step) % count) for place in ra...  4.74 us
  transfers between devices with their start and end apart: 19, of which 12 were waited for; matrix products, arithmetic and copies ran while one was open for 6% of the time, Pallas kernels for 25%

profile of v2, /device:TPU:18, one launch (start us, length us, event | category | flops | bytes accessed | tf_op | source)
XLA Modules:
  0.0 212.3 jit_solution(6303020220645094627)
XLA Ops:
  0.6 0.8 constant_dynamic-update-slice_fusion.15
  1.4 0.8 constant_dynamic-update-slice_fusion.14
  2.2 0.8 constant_dynamic-update-slice_fusion.13
  3.0 0.8 constant_dynamic-update-slice_fusion.12
  3.8 0.8 constant_dynamic-update-slice_fusion.11
  4.6 0.8 constant_dynamic-update-slice_fusion.10
  5.4 0.8 constant_dynamic-update-slice_fusion.9
  6.2 0.8 constant_dynamic-update-slice_fusion.8
  7.0 0.8 constant_dynamic-update-slice_fusion.1
  7.8 0.8 constant_dynamic-update-slice_fusion
  8.6 1.6 collective-permute-start
  10.1 6.5 %collective-permute-done = bf16[128,1024]{1,0:T(8,128)(2,1)S(1)} collective-permute-done((bf16[128,1024]{1,0:T(8,128)(2,1)S(1)}, bf16[128,1024]{1,0:T(8,128)(2,1)S(1)}, u32[]{:S(2)}, u32[]{:S(2)}) %collective-permute-start) | collective-permute-done | bytes 262176 | tf_op jit(solution)/shard_map/ppermute | solution.py:164
  16.8 3.5 %collective-permute-start.5 = (bf16[256,512]{1,0:T(8,128)(2,1)S(1)}, bf16[256,512]{1,0:T(8,128)(2,1)S(1)}, u32[]{:S(2)}, u32[]{:S(2)}) collective-permute-start(bf16[256,512]{1,0:T(8,128)(2,1)S(1)} %get-tuple-element.30.own_ref), channel_id=1, source_target_pairs={{0,8},{2,10},{4,12},{6,14},{8,16},{10,18},{12,20},{14,22},{16,24},... | collective-permute-start | bytes 786440 | tf_op jit(solution)/shard_map/ppermute | solution.py:151
  20.3 5.6 %collective-permute-done.5.far_ref = bf16[256,512]{1,0:T(8,128)(2,1)S(1)} collective-permute-done((bf16[256,512]{1,0:T(8,128)(2,1)S(1)}, bf16[256,512]{1,0:T(8,128)(2,1)S(1)}, u32[]{:S(2)}, u32[]{:S(2)}) %collective-permute-start.5) | collective-permute-done | bytes 262176 | tf_op jit(solution)/shard_map/ppermute | solution.py:151
  25.9 3.5 %collective-permute-start.6 = (bf16[256,512]{1,0:T(8,128)(2,1)S(1)}, bf16[256,512]{1,0:T(8,128)(2,1)S(1)}, u32[]{:S(2)}, u32[]{:S(2)}) collective-permute-start(bf16[256,512]{1,0:T(8,128)(2,1)S(1)} %collective-permute-done.5.far_ref), channel_id=1, source_target_pairs={{0,8},{2,10},{4,12},{6,14},{8,16},{10,18},{12,20},{14,22},{16,24},... | collective-permute-start | bytes 786440 | tf_op jit(solution)/shard_map/ppermute | solution.py:151
  29.4 1.9 collective-permute-start.1
  31.3 5.3 %collective-permute-done.6 = bf16[256,512]{1,0:T(8,128)(2,1)S(1)} collective-permute-done((bf16[256,512]{1,0:T(8,128)(2,1)S(1)}, bf16[256,512]{1,0:T(8,128)(2,1)S(1)}, u32[]{:S(2)}, u32[]{:S(2)}) %collective-permute-start.6) | collective-permute-done | bytes 262176 | tf_op jit(solution)/shard_map/ppermute | solution.py:151
  37.3 2.4 %collective-permute-done.1.far_ref = bf16[256,512]{1,0:T(8,128)(2,1)S(1)} collective-permute-done((bf16[256,512]{1,0:T(8,128)(2,1)S(1)}, bf16[256,512]{1,0:T(8,128)(2,1)S(1)}, u32[]{:S(2)}, u32[]{:S(2)}) %collective-permute-start.1) | collective-permute-done | bytes 262176 | tf_op jit(solution)/shard_map/ppermute | solution.py:151
  39.7 3.4 %collective-permute-start.2 = (bf16[256,512]{1,0:T(8,128)(2,1)S(1)}, bf16[256,512]{1,0:T(8,128)(2,1)S(1)}, u32[]{:S(2)}, u32[]{:S(2)}) collective-permute-start(bf16[256,512]{1,0:T(8,128)(2,1)S(1)} %collective-permute-done.1.far_ref), channel_id=1, source_target_pairs={{0,8},{2,10},{4,12},{6,14},{8,16},{10,18},{12,20},{14,22},{16,24},... | collective-permute-start | bytes 786440 | tf_op jit(solution)/shard_map/ppermute | solution.py:151
  43.3 4.7 %collective-permute-done.2 = bf16[256,512]{1,0:T(8,128)(2,1)S(1)} collective-permute-done((bf16[256,512]{1,0:T(8,128)(2,1)S(1)}, bf16[256,512]{1,0:T(8,128)(2,1)S(1)}, u32[]{:S(2)}, u32[]{:S(2)}) %collective-permute-start.2) | collective-permute-done | bytes 262176 | tf_op jit(solution)/shard_map/ppermute | solution.py:151
  52.7 0.7 pad_add_fusion.info
  53.4 9.9 %collective-permute-done.3.x_ref = bf16[2,256,512]{2,1,0:T(8,128)(2,1)S(1)} collective-permute-done((bf16[2,256,512]{2,1,0:T(8,128)(2,1)S(1)}, bf16[2,256,512]{2,1,0:T(8,128)(2,1)S(1)}, u32[]{:S(2)}, u32[]{:S(2)}) %collective-permute-start.3) | collective-permute-done | bytes 524320 | tf_op jit(solution)/shard_map/ppermute | solution.py:155
  64.1 0.8 broadcast_in_dim.13.low_ref
  64.9 26.6 %attend_groups_0.1 = (bf16[256,4096]{1,0:T(8,128)(2,1)}, bf16[256,4096]{1,0:T(8,128)(2,1)}, bf16[4,256,512]{2,1,0:T(8,128)(2,1)}, bf16[4,256,512]{2,1,0:T(8,128)(2,1)}) custom-call(s32[2]{0:T(128)} %pad_add_fusion.info, bf16[256,4096]{1,0:T(8,128)(2,1)} %q_ref.3, bf16[256,4096]{1,0:T(8,128)(2,1)} %g_ref.3, bf16[256,512]{1,0:T(8,128)(2,1)} %copy-done.6, ...), custom_call_target="tpu_custom_call" | custom-call | flops 12884901888 | bytes 8388608 | tf_op jit(solution)/shard_map/attend_groups_0/pallas_call | solution.py:114
  92.0 1.0 copy-done.14
  93.0 26.6 %attend_groups_2.1 = (bf16[256,4096]{1,0:T(8,128)(2,1)}, bf16[256,4096]{1,0:T(8,128)(2,1)}, bf16[4,256,512]{2,1,0:T(8,128)(2,1)}, bf16[4,256,512]{2,1,0:T(8,128)(2,1)}) custom-call(s32[2]{0:T(128)} %pad_add_fusion.info, bf16[256,4096]{1,0:T(8,128)(2,1)} %q_ref.3, bf16[256,4096]{1,0:T(8,128)(2,1)} %g_ref.3, ...), custom_call_target="tpu_custom_call", output_to_operand_aliasing={{0}: (8, {}), {1}: (9, {})} | custom-call | flops 12884901888 | bytes 8388608 | tf_op jit(solution)/shard_map/attend_groups_2/pallas_call | solution.py:114
  119.7 1.6 convert_element_type.65
  122.3 0.8 copy-done.4
  123.2 34.5 %collective-permute-start.10 = (bf16[2,256,512]{2,1,0:T(8,128)(2,1)S(1)}, bf16[2,256,512]{2,1,0:T(8,128)(2,1)S(1)}, u32[]{:S(2)}, u32[]{:S(2)}) collective-permute-start(bf16[2,256,512]{2,1,0:T(8,128)(2,1)S(1)} %pad_maximum_fusion.4), channel_id=1, source_target_pairs={{0,4},{2,6},{4,0},{6,2},{8,12},{10,14},{12,8},{14,10},{16,20},{18,... | collective-permute-start | bytes 1572872 | tf_op jit(solution)/shard_map/ppermute | solution.py:155
  158.4 1.1 pad_maximum_fusion.5
  159.6 10.9 %collective-permute-done.10 = bf16[2,256,512]{2,1,0:T(8,128)(2,1)S(1)} collective-permute-done((bf16[2,256,512]{2,1,0:T(8,128)(2,1)S(1)}, bf16[2,256,512]{2,1,0:T(8,128)(2,1)S(1)}, u32[]{:S(2)}, u32[]{:S(2)}) %collective-permute-start.10) | collective-permute-done | bytes 524320 | tf_op jit(solution)/shard_map/ppermute | solution.py:155
  170.6 0.8 fusion.20
  171.5 1.9 collective-permute-start.11
  173.4 8.2 %collective-permute-done.15 = bf16[2,256,512]{2,1,0:T(8,128)(2,1)} collective-permute-done((bf16[2,256,512]{2,1,0:T(8,128)(2,1)}, bf16[2,256,512]{2,1,0:T(8,128)(2,1)}, u32[]{:S(2)}, u32[]{:S(2)}) %collective-permute-start.15) | collective-permute-done | bytes 524320 | tf_op jit(solution)/shard_map/ppermute | solution.py:155
  181.6 1.2 convert_element_type.67
  182.8 1.3 fusion.21
  184.1 2.1 collective-permute-start.16
  186.2 1.4 fusion.13
  187.5 1.9 collective-permute-start.12
  189.5 6.4 %collective-permute-done.16 = bf16[256,512]{1,0:T(8,128)(2,1)S(1)} collective-permute-done((bf16[256,512]{1,0:T(8,128)(2,1)S(1)}, bf16[256,512]{1,0:T(8,128)(2,1)S(1)}, u32[]{:S(2)}, u32[]{:S(2)}) %collective-permute-start.16) | collective-permute-done | bytes 262176 | tf_op jit(solution)/shard_map/ppermute | solution.py:151
  196.2 1.9 collective-permute-start.17
  198.1 3.4 %collective-permute-done.12 = bf16[256,512]{1,0:T(8,128)(2,1)S(1)} collective-permute-done((bf16[256,512]{1,0:T(8,128)(2,1)S(1)}, bf16[256,512]{1,0:T(8,128)(2,1)S(1)}, u32[]{:S(2)}, u32[]{:S(2)}) %collective-permute-start.12) | collective-permute-done | bytes 262176 | tf_op jit(solution)/shard_map/ppermute | solution.py:151
  201.4 1.3 fusion.19
  202.7 1.6 collective-permute-start.13
  204.3 1.7 collective-permute-done.17
  206.2 1.6 collective-permute-start.18
  207.9 3.3 %collective-permute-done.18 = bf16[128,512]{1,0:T(8,128)(2,1)S(1)} collective-permute-done((bf16[128,512]{1,0:T(8,128)(2,1)S(1)}, bf16[128,512]{1,0:T(8,128)(2,1)S(1)}, u32[]{:S(2)}, u32[]{:S(2)}) %collective-permute-start.18) | collective-permute-done | bytes 131104 | tf_op jit(solution)/shard_map/ppermute | solution.py:164
  211.5 0.7 copy-done.12
  (79 shorter events, 7.2 us)
Async XLA Ops:
  8.6 8.1 %collective-permute-start = (bf16[128,1024]{1,0:T(8,128)(2,1)S(1)}, bf16[128,1024]{1,0:T(8,128)(2,1)S(1)}, u32[]{:S(2)}, u32[]{:S(2)}) collective-permute-start(bf16[128,1024]{1,0:T(8,128)(2,1)S(1)} %constant_dynamic-update-slice_fusion), channel_id=1, source_target_pairs={{0,1},{1,0},{2,3},{3,2},{4,5},{5,4},{6,7},{7,6},{8,9},{9,8},{10,11... | collective-permute-start | bytes 786440 | tf_op jit(solution)/shard_map/ppermute | solution.py:164
  16.7 26.4 %copy-start.15 = (s32[8]{0:T(128)S(1)}, s32[8]{0:T(128)}, u32[]{:S(2)}) copy-start(s32[8]{0:T(128)} %param.9) | copy-start | bytes 100
  16.8 31.4 %copy-start.6 = (bf16[256,512]{1,0:T(8,128)(2,1)}, bf16[256,512]{1,0:T(8,128)(2,1)S(1)}, u32[]{:S(2)}) copy-start(bf16[256,512]{1,0:T(8,128)(2,1)S(1)} %get-tuple-element.30.own_ref) | copy-start | bytes 786436
  16.8 46.5 %copy-start.5 = (bf16[256,512]{1,0:T(8,128)(2,1)}, bf16[256,512]{1,0:T(8,128)(2,1)S(1)}, u32[]{:S(2)}) copy-start(bf16[256,512]{1,0:T(8,128)(2,1)S(1)} %get-tuple-element.31.own_ref) | copy-start | bytes 786436
  16.8 9.1 %collective-permute-start.5 = (bf16[256,512]{1,0:T(8,128)(2,1)S(1)}, bf16[256,512]{1,0:T(8,128)(2,1)S(1)}, u32[]{:S(2)}, u32[]{:S(2)}) collective-permute-start(bf16[256,512]{1,0:T(8,128)(2,1)S(1)} %get-tuple-element.30.own_ref), channel_id=1, source_target_pairs={{0,8},{2,10},{4,12},{6,14},{8,16},{10,18},{12,20},{14,22},{16,24},... | collective-permute-start | bytes 786440 | tf_op jit(solution)/shard_map/ppermute | solution.py:151
  25.8 22.3 %copy-start.8 = (bf16[256,512]{1,0:T(8,128)(2,1)}, bf16[256,512]{1,0:T(8,128)(2,1)S(1)}, u32[]{:S(2)}) copy-start(bf16[256,512]{1,0:T(8,128)(2,1)S(1)} %collective-permute-done.5.far_ref) | copy-start | bytes 786436
  25.9 10.7 %collective-permute-start.6 = (bf16[256,512]{1,0:T(8,128)(2,1)S(1)}, bf16[256,512]{1,0:T(8,128)(2,1)S(1)}, u32[]{:S(2)}, u32[]{:S(2)}) collective-permute-start(bf16[256,512]{1,0:T(8,128)(2,1)S(1)} %collective-permute-done.5.far_ref), channel_id=1, source_target_pairs={{0,8},{2,10},{4,12},{6,14},{8,16},{10,18},{12,20},{14,22},{16,24},... | collective-permute-start | bytes 786440 | tf_op jit(solution)/shard_map/ppermute | solution.py:151
  29.4 10.4 %collective-permute-start.1 = (bf16[256,512]{1,0:T(8,128)(2,1)S(1)}, bf16[256,512]{1,0:T(8,128)(2,1)S(1)}, u32[]{:S(2)}, u32[]{:S(2)}) collective-permute-start(bf16[256,512]{1,0:T(8,128)(2,1)S(1)} %get-tuple-element.31.own_ref), channel_id=1, source_target_pairs={{0,8},{2,10},{4,12},{6,14},{8,16},{10,18},{12,20},{14,22},{16,24},... | collective-permute-start | bytes 786440 | tf_op jit(solution)/shard_map/ppermute | solution.py:151
  36.7 11.3 %collective-permute-start.7 = (bf16[2,256,512]{2,1,0:T(8,128)(2,1)S(1)}, bf16[2,256,512]{2,1,0:T(8,128)(2,1)S(1)}, u32[]{:S(2)}, u32[]{:S(2)}) collective-permute-start(bf16[2,256,512]{2,1,0:T(8,128)(2,1)S(1)} %pad_maximum_fusion.3), channel_id=1, source_target_pairs={{0,4},{2,6},{4,0},{6,2},{8,12},{10,14},{12,8},{14,10},{16,20},{18,... | collective-permute-start | bytes 1572872 | tf_op jit(solution)/shard_map/ppermute | solution.py:155
  39.7 23.6 %copy-start.9 = (bf16[256,512]{1,0:T(8,128)(2,1)}, bf16[256,512]{1,0:T(8,128)(2,1)S(1)}, u32[]{:S(2)}) copy-start(bf16[256,512]{1,0:T(8,128)(2,1)S(1)} %collective-permute-done.1.far_ref) | copy-start | bytes 786436
  39.7 8.3 %collective-permute-start.2 = (bf16[256,512]{1,0:T(8,128)(2,1)S(1)}, bf16[256,512]{1,0:T(8,128)(2,1)S(1)}, u32[]{:S(2)}, u32[]{:S(2)}) collective-permute-start(bf16[256,512]{1,0:T(8,128)(2,1)S(1)} %collective-permute-done.1.far_ref), channel_id=1, source_target_pairs={{0,8},{2,10},{4,12},{6,14},{8,16},{10,18},{12,20},{14,22},{16,24},... | collective-permute-start | bytes 786440 | tf_op jit(solution)/shard_map/ppermute | solution.py:151
  48.0 0.8 copy-start.10
  48.8 15.3 %collective-permute-start.8 = (bf16[4,256,512]{2,1,0:T(8,128)(2,1)S(1)}, bf16[4,256,512]{2,1,0:T(8,128)(2,1)}, u32[]{:S(2)}, u32[]{:S(2)}) collective-permute-start(bf16[4,256,512]{2,1,0:T(8,128)(2,1)S(1)} %pad_maximum_fusion.1), channel_id=1, source_target_pairs={{0,2},{2,0},{4,6},{6,4},{8,10},{10,8},{12,14},{14,12},{16,18},{18,... | collective-permute-start | bytes 3145736 | tf_op jit(solution)/shard_map/ppermute | solution.py:155
  48.9 14.4 %collective-permute-start.3 = (bf16[2,256,512]{2,1,0:T(8,128)(2,1)S(1)}, bf16[2,256,512]{2,1,0:T(8,128)(2,1)S(1)}, u32[]{:S(2)}, u32[]{:S(2)}) collective-permute-start(bf16[2,256,512]{2,1,0:T(8,128)(2,1)S(1)} %pad_maximum_fusion.2), channel_id=1, source_target_pairs={{0,4},{2,6},{4,0},{6,2},{8,12},{10,14},{12,8},{14,10},{16,20},{18,... | collective-permute-start | bytes 1572872 | tf_op jit(solution)/shard_map/ppermute | solution.py:155
  63.3 0.8 copy-start.11
  64.1 27.9 %collective-permute-start.4 = (bf16[4,256,512]{2,1,0:T(8,128)(2,1)S(1)}, bf16[4,256,512]{2,1,0:T(8,128)(2,1)S(1)}, u32[]{:S(2)}, u32[]{:S(2)}) collective-permute-start(bf16[4,256,512]{2,1,0:T(8,128)(2,1)S(1)} %pad_maximum_fusion), channel_id=1, source_target_pairs={{0,2},{2,0},{4,6},{6,4},{8,10},{10,8},{12,14},{14,12},{16,18},{18,... | collective-permute-start | bytes 3145736 | tf_op jit(solution)/shard_map/ppermute | solution.py:155
  91.5 30.1 %collective-permute-start.9 = (bf16[4,256,512]{2,1,0:T(8,128)(2,1)}, bf16[4,256,512]{2,1,0:T(8,128)(2,1)S(1)}, u32[]{:S(2)}, u32[]{:S(2)}) collective-permute-start(bf16[4,256,512]{2,1,0:T(8,128)(2,1)} %get-tuple-element.17), channel_id=1, source_target_pairs={{0,2},{2,0},{4,6},{6,4},{8,10},{10,8},{12,14},{14,12},{16,18},{18,... | collective-permute-start | bytes 3145736 | tf_op jit(solution)/shard_map/ppermute | solution.py:155
  92.0 1.0 copy-start.14
  119.6 1.7 copy-start.7
  119.6 38.1 %collective-permute-start.14 = (bf16[4,256,512]{2,1,0:T(8,128)(2,1)}, bf16[4,256,512]{2,1,0:T(8,128)(2,1)S(1)}, u32[]{:S(2)}, u32[]{:S(2)}) collective-permute-start(bf16[4,256,512]{2,1,0:T(8,128)(2,1)} %get-tuple-element.19), channel_id=1, source_target_pairs={{0,2},{2,0},{4,6},{6,4},{8,10},{10,8},{12,14},{14,12},{16,18},{18,... | collective-permute-start | bytes 3145736 | tf_op jit(solution)/shard_map/ppermute | solution.py:155
  121.3 36.7 %copy-start.2 = (f32[4,256,512]{2,1,0:T(8,128)}, f32[4,256,512]{2,1,0:T(8,128)S(1)}, u32[]{:S(2)}) copy-start(f32[4,256,512]{2,1,0:T(8,128)S(1)} %convert_element_type.65) | copy-start | bytes 6291460
  121.6 1.5 copy-start.4
  123.2 47.3 %collective-permute-start.10 = (bf16[2,256,512]{2,1,0:T(8,128)(2,1)S(1)}, bf16[2,256,512]{2,1,0:T(8,128)(2,1)S(1)}, u32[]{:S(2)}, u32[]{:S(2)}) collective-permute-start(bf16[2,256,512]{2,1,0:T(8,128)(2,1)S(1)} %pad_maximum_fusion.4), channel_id=1, source_target_pairs={{0,4},{2,6},{4,0},{6,2},{8,12},{10,14},{12,8},{14,10},{16,20},{18,... | collective-permute-start | bytes 1572872 | tf_op jit(solution)/shard_map/ppermute | solution.py:155
  158.0 1.5 copy-start
  159.6 22.0 %collective-permute-start.15 = (bf16[2,256,512]{2,1,0:T(8,128)(2,1)}, bf16[2,256,512]{2,1,0:T(8,128)(2,1)}, u32[]{:S(2)}, u32[]{:S(2)}) collective-permute-start(bf16[2,256,512]{2,1,0:T(8,128)(2,1)} %pad_maximum_fusion.5), channel_id=1, source_target_pairs={{0,4},{2,6},{4,0},{6,2},{8,12},{10,14},{12,8},{14,10},{16,20},{18,... | collective-permute-start | bytes 1572872 | tf_op jit(solution)/shard_map/ppermute | solution.py:155
  171.5 14.7 %collective-permute-start.11 = (bf16[256,512]{1,0:T(8,128)(2,1)}, bf16[256,512]{1,0:T(8,128)(2,1)S(1)}, u32[]{:S(2)}, u32[]{:S(2)}) collective-permute-start(bf16[256,512]{1,0:T(8,128)(2,1)} %fusion.20), channel_id=1, source_target_pairs={{8,0},{10,2},{12,4},{14,6},{16,8},{18,10},{20,12},{22,14},{24,16},... | collective-permute-start | bytes 786440 | tf_op jit(solution)/shard_map/ppermute | solution.py:151
  182.8 13.1 %copy-start.1 = (f32[4,256,512]{2,1,0:T(8,128)S(1)}, f32[4,256,512]{2,1,0:T(8,128)}, u32[]{:S(2)}) copy-start(f32[4,256,512]{2,1,0:T(8,128)} %copy-done) | copy-start | bytes 6291460
  182.8 13.1 %copy-start.3 = (f32[4,256,512]{2,1,0:T(8,128)S(1)}, f32[4,256,512]{2,1,0:T(8,128)}, u32[]{:S(2)}) copy-start(f32[4,256,512]{2,1,0:T(8,128)} %copy-done.2) | copy-start | bytes 6291460
  184.1 11.7 %collective-permute-start.16 = (bf16[256,512]{1,0:T(8,128)(2,1)S(1)}, bf16[256,512]{1,0:T(8,128)(2,1)S(1)}, u32[]{:S(2)}, u32[]{:S(2)}) collective-permute-start(bf16[256,512]{1,0:T(8,128)(2,1)S(1)} %fusion.21), channel_id=1, source_target_pairs={{8,0},{10,2},{12,4},{14,6},{16,8},{18,10},{20,12},{22,14},{24,16},... | collective-permute-start | bytes 786440 | tf_op jit(solution)/shard_map/ppermute | solution.py:151
  187.5 13.9 %collective-permute-start.12 = (bf16[256,512]{1,0:T(8,128)(2,1)S(1)}, bf16[256,512]{1,0:T(8,128)(2,1)S(1)}, u32[]{:S(2)}, u32[]{:S(2)}) collective-permute-start(bf16[256,512]{1,0:T(8,128)(2,1)S(1)} %fusion.13), channel_id=1, source_target_pairs={{8,0},{10,2},{12,4},{14,6},{16,8},{18,10},{20,12},{22,14},{24,16},... | collective-permute-start | bytes 786440 | tf_op jit(solution)/shard_map/ppermute | solution.py:151
  196.2 9.8 %collective-permute-start.17 = (bf16[256,512]{1,0:T(8,128)(2,1)S(1)}, bf16[256,512]{1,0:T(8,128)(2,1)S(1)}, u32[]{:S(2)}, u32[]{:S(2)}) collective-permute-start(bf16[256,512]{1,0:T(8,128)(2,1)S(1)} %fusion.3), channel_id=1, source_target_pairs={{8,0},{10,2},{12,4},{14,6},{16,8},{18,10},{20,12},{22,14},{24,16},... | collective-permute-start | bytes 786440 | tf_op jit(solution)/shard_map/ppermute | solution.py:151
  202.7 5.1 %collective-permute-start.13 = (bf16[128,512]{1,0:T(8,128)(2,1)S(1)}, bf16[128,512]{1,0:T(8,128)(2,1)S(1)}, u32[]{:S(2)}, u32[]{:S(2)}) collective-permute-start(bf16[128,512]{1,0:T(8,128)(2,1)S(1)} %constant_dynamic-slice_fusion.1), channel_id=1, source_target_pairs={{0,1},{1,0},{2,3},{3,2},{4,5},{5,4},{6,7},{7,6},{8,9},{9,8},{10,11... | collective-permute-start | bytes 393224 | tf_op jit(solution)/shard_map/ppermute | solution.py:164
  206.2 5.0 %collective-permute-start.18 = (bf16[128,512]{1,0:T(8,128)(2,1)S(1)}, bf16[128,512]{1,0:T(8,128)(2,1)S(1)}, u32[]{:S(2)}, u32[]{:S(2)}) collective-permute-start(bf16[128,512]{1,0:T(8,128)(2,1)S(1)} %constant_dynamic-slice_fusion), channel_id=1, source_target_pairs={{0,1},{1,0},{2,3},{3,2},{4,5},{5,4},{6,7},{7,6},{8,9},{9,8},{10,11... | collective-permute-start | bytes 393224 | tf_op jit(solution)/shard_map/ppermute | solution.py:164
  211.5 0.7 copy-start.12
  211.5 0.8 copy-start.13
